TPU v7x, 32 devices: a whole 2x2x4 slice. The times are simulated.
32 devices in a mesh: layer: 4 (over y, x), latent: 8 (over z, core).
Axes of the slice: x: 2, y: 2, z: 4, core: 2. Of those that a mesh axis runs over, the one named last changes fastest.
Arguments:
- residual: bfloat16 [4, 512, 1792], P('layer', 'latent'), may hold values from -6 to 6
- target: bfloat16 [4, 512, 1792], P('layer', 'latent'), may hold values from -6 to 6
- enc_weight: bfloat16 [4, 1792, 2048], P('layer', None, 'latent'), may hold values from -0.125 to 0.125
- enc_bias: float32 [4, 2048], P('layer', 'latent'), may hold values from -3 to 3
- dec_weight: bfloat16 [4, 4, 2048, 1792], P(None, 'layer', 'latent'), may hold values from -0.1875 to 0.1875
- active: int32 [4, 8, 4], replicated, may hold values from 0 to 7, all different within a row; in each aligned block of 8 rows (0 to 7, 8 to 15, ..., all dimensions but the last counted through in order) at most 6 rows name the same one
Outputs:
- loss: float32 [], replicated
- enc_grad: bfloat16 [4, 1792, 2048], P('layer', None, 'latent')
- bias_grad: float32 [4, 2048], P('layer', 'latent')
- dec_grad: bfloat16 [4, 4, 2048, 1792], P(None, 'layer', 'latent')
Inputs may be any that keep to these rules, and one draw needn't show every extreme that they name: `active`: each row lists 4 different blocks of its layer; within one layer no block is listed on more than 6 token tiles, and in every draw some block of some layer is listed on exactly 6.
All inputs are finite; a program needn't handle non-finite values.
Results may differ from a plain program's by a relative error of at most 0.023.
Values may be sent and summed in bfloat16 or wider, within the bound.
A program may use at most 128 MiB of HBM per device.

v0:
```python
import jax
import jax.numpy as jnp
from jax import lax
from jax.sharding import PartitionSpec as P

D = 1792
BLOCK = 256
TILE = 64
NTILE = 8
CAP = 6


def shifted(value, axis, steps):
    count = lax.axis_size(axis)
    leading, last = (max(0, -steps), min(count, count - steps))
    return lax.ppermute(value, axis, [(source, source + steps) for source in range(leading, last)])


def slot_list(active, layer, my_block, slot_count):
    block_ids = lax.dynamic_index_in_dim(active, layer, 0, keepdims=False)
    hit = jnp.any(block_ids == my_block, axis=1).astype(jnp.int32)
    every = jnp.arange(NTILE, dtype=jnp.int32)
    place = jnp.cumsum(hit) - 1
    chosen = (hit[None, :] == 1) & (
        place[None, :] == jnp.arange(slot_count, dtype=jnp.int32)[:, None]
    )
    tile_ids = jnp.sum(jnp.where(chosen, every[None, :], 0), axis=1)
    filled = jnp.sum(chosen.astype(jnp.float32), axis=1)
    return (tile_ids, filled)


def shards(residual, target, enc_weight, enc_bias, dec_weight, active):
    layers = dec_weight.shape[0]
    feat_dev = enc_weight.shape[2]
    layer_index = lax.axis_index("layer")
    my_block = lax.axis_index("latent") * feat_dev // BLOCK
    slot_count = CAP
    slot_rows = slot_count * TILE
    full_inputs = lax.all_gather(residual[0], "latent", axis=0, tiled=True).reshape(NTILE, TILE, D)
    own_tiles, own_filled = slot_list(active, layer_index, my_block, slot_count)
    rows = jnp.take(full_inputs, own_tiles, axis=0).reshape(slot_rows, D)
    preact = jnp.dot(rows, enc_weight[0], preferred_element_type=jnp.float32) + enc_bias[0][None, :]
    live = jnp.repeat(own_filled, TILE)[:, None]
    sparse_codes = (jnp.maximum(preact, 0.0) * live).astype(jnp.bfloat16)
    dec_all = dec_weight[:, 0]

    def take_source(carry, portion, source):
        writes, kept = carry
        usable = (source >= 0) & (source <= layer_index)
        source_idx = jnp.clip(source, 0, layers - 1)
        portion = jnp.where(usable, portion, jnp.zeros_like(portion))
        tile_ids, _ = slot_list(active, source_idx, my_block, slot_count)
        weight = lax.dynamic_index_in_dim(dec_all, source_idx, 0, keepdims=False)
        product = jnp.dot(portion, weight, preferred_element_type=jnp.float32).reshape(
            slot_count, TILE, D
        )
        writes = writes.at[tile_ids].add(product)
        kept = jnp.where(usable, kept.at[source_idx].set(portion), kept)
        return (writes, kept)

    start_state = (
        jnp.zeros((NTILE, TILE, D), jnp.float32),
        jnp.zeros((layers, slot_rows, feat_dev), jnp.bfloat16),
    )
    state = take_source(start_state, sparse_codes, layer_index)
    moving = sparse_codes
    for hop in range(1, layers):
        moving = shifted(moving, "layer", 1)
        state = take_source(state, moving, layer_index - hop)
    writes, kept = state
    recon = lax.psum_scatter(
        writes.reshape(NTILE * TILE, D), "latent", scatter_dimension=0, tiled=True
    )
    errors = recon - target[0].astype(jnp.float32)
    total = lax.psum(jnp.sum(errors * errors), ("layer", "latent"))
    loss = 0.5 * total / (layers * NTILE * TILE * D)
    full_errors = lax.all_gather(errors.astype(jnp.bfloat16), "latent", axis=0, tiled=True).reshape(
        NTILE, TILE, D
    )
    dec_grads = []
    code_grads = []
    for source in range(layers):
        tile_ids, _ = slot_list(active, source, my_block, slot_count)
        error_part = jnp.take(full_errors, tile_ids, axis=0).reshape(slot_rows, D)
        grad = lax.dot_general(
            kept[source], error_part, (((0,), (0,)), ((), ())), preferred_element_type=jnp.float32
        )
        dec_grads.append((grad / TILE).astype(jnp.bfloat16))
        back = lax.dot_general(
            error_part,
            dec_all[source],
            (((1,), (1,)), ((), ())),
            preferred_element_type=jnp.float32,
        )
        code_grads.append(jnp.where(source <= layer_index, back, jnp.zeros_like(back)))
    dec_grad = jnp.stack(dec_grads)[:, None]
    code_grad = jnp.stack(code_grads)
    running = code_grad
    for hop in range(1, layers):
        running = code_grad + shifted(running, "layer", -1)
    mine = lax.dynamic_index_in_dim(running, layer_index, 0, keepdims=False)
    pre_grad = jnp.where(preact > 0, mine, jnp.zeros_like(mine)) * live
    bias_grad = (jnp.sum(pre_grad, axis=0) / TILE)[None]
    enc_term = lax.dot_general(
        rows,
        pre_grad.astype(jnp.bfloat16),
        (((0,), (0,)), ((), ())),
        preferred_element_type=jnp.float32,
    )
    enc_grad = (enc_term / TILE).astype(jnp.bfloat16)[None]
    return (loss, enc_grad, bias_grad, dec_grad)


def solution(mesh):
    in_specs = (
        P("layer", "latent", None),
        P("layer", "latent", None),
        P("layer", None, "latent"),
        P("layer", "latent"),
        P(None, "layer", "latent", None),
        P(),
    )
    out_specs = (
        P(),
        P("layer", None, "latent"),
        P("layer", "latent"),
        P(None, "layer", "latent", None),
    )
    return jax.shard_map(shards, mesh=mesh, in_specs=in_specs, out_specs=out_specs, check_vma=False)
```

profile of v0, /device:TPU:0, one launch (start us, length us, event | category | flops | bytes accessed | tf_op | source)
XLA Modules:
  0.0 361.6 jit_solution(859726386251682435)
XLA Ops:
  7.2 0.7 all-gather.6.cloned.1.call-update
  8.0 0.9 fusion.61
  10.8 1.5 and_reduce_fusion
  12.3 27.0 %all-gather.6.cloned.1.call-done = bf16[1,512,1792]{2,1,0:T(8,128)(2,1)} async-done(((bf16[1,64,1792]{2,1,0:T(8,128)(2,1)}), bf16[1,512,1792]{2,1,0:T(8,128)(2,1)}) %all-gather.6.cloned.1.call-update) | async-done | bytes 1835024 | tf_op jit(solution)/shard_map/all_gather | solution.py:39
  39.3 2.1 gather_fusion
  41.5 0.2 broadcast_select_fusion.4
  41.7 0.4 copy-done.27
  42.1 1.9 bitcast_dynamic-update-slice_fusion
  44.1 3.4 collective-permute-start
  47.5 3.3 fusion.20
  50.7 2.1 broadcast_in_dim.129
  52.9 8.0 %scatter_fusion = f32[8,64,1792]{2,1,0:T(8,128)} fusion(f32[8,64,1792]{2,1,0:T(8,128)} %broadcast_in_dim.129, s32[6]{0:T(128)S(1)} %get-tuple-element.105, f32[6,64,1792]{2,1,0:T(8,128)} %fusion.20), kind=kCustom, calls=%fused_computation.5 | custom fusion | flops 688128 | bytes 8257560 | tf_op jit(solution)/shard_map/scatter-add | solution.py:57
  60.9 3.5 collective-permute-start.1
  64.5 3.3 fusion.18
  67.7 8.0 %scatter_fusion.1 = f32[8,64,1792]{2,1,0:T(8,128)} fusion(f32[8,64,1792]{2,1,0:T(8,128)} %scatter_fusion, s32[6]{0:T(128)S(1)} %fusion.71, f32[6,64,1792]{2,1,0:T(8,128)} %fusion.18), kind=kCustom, calls=%fused_computation.6 | custom fusion | flops 688128 | bytes 8257560 | tf_op jit(solution)/shard_map/scatter-add | solution.py:57
  75.7 3.2 collective-permute-start.2
  79.0 3.3 fusion.16
  82.3 8.0 %scatter_fusion.2 = f32[8,64,1792]{2,1,0:T(8,128)} fusion(f32[8,64,1792]{2,1,0:T(8,128)} %scatter_fusion.1, s32[6]{0:T(128)S(1)} %fusion.72, f32[6,64,1792]{2,1,0:T(8,128)} %fusion.16), kind=kCustom, calls=%fused_computation.7 | custom fusion | flops 688128 | bytes 8257560 | tf_op jit(solution)/shard_map/scatter-add | solution.py:57
  90.3 3.3 fusion.14
  93.7 8.0 %scatter_fusion.3 = f32[8,64,1792]{2,1,0:T(8,128)} fusion(f32[8,64,1792]{2,1,0:T(8,128)} %scatter_fusion.2, s32[6]{0:T(128)S(1)} %get-tuple-element.106, f32[6,64,1792]{2,1,0:T(8,128)} %fusion.14), kind=kCustom, calls=%fused_computation.8 | custom fusion | flops 688128 | bytes 8257560 | tf_op jit(solution)/shard_map/scatter-add | solution.py:57
  102.0 43.2 %reduce-scatter.2.cloned.1.call-done = f32[64,1792]{1,0:T(8,128)} async-done(((f32[512,1792]{1,0:T(8,128)}), f32[64,1792]{1,0:T(8,128)}) %reduce-scatter.2.cloned.1.call-update) | async-done | bytes 458768 | tf_op jit(solution)/shard_map/reduce_scatter | solution.py:71
  145.2 2.4 fusion.38
  148.6 0.6 pad_clamp_fusion
  149.2 0.6 compare_and_fusion.3
  149.8 0.5 compare_and_fusion.2
  150.4 0.6 compare_and_fusion.1
  150.9 0.6 compare_and_fusion
  151.5 21.6 %all-gather.4.cloned.1.call-done = bf16[512,1792]{1,0:T(8,128)(2,1)} async-done(((bf16[64,1792]{1,0:T(8,128)(2,1)}), bf16[512,1792]{1,0:T(8,128)(2,1)}) %all-gather.4.cloned.1.call-update) | async-done | bytes 1835024 | tf_op jit(solution)/shard_map/all_gather | solution.py:77
  173.1 3.4 gather_fusion.1
  176.5 1.8 gather_fusion.2
  178.3 1.8 gather_fusion.3
  180.0 2.0 gather_fusion.4
  182.1 1.5 broadcast_select_fusion.3
  183.6 1.8 fusion.13
  185.7 1.1 copy-done.9
  186.8 0.2 broadcast_select_fusion.1
  187.0 1.6 copy-done.8
  188.9 1.3 copy-done.11
  190.2 0.6 fusion.11
  190.7 0.6 fusion.12
  191.3 0.6 fusion.10
  192.0 1.1 copy-done.12
  193.1 1.4 collective-permute-start.3
  194.6 37.1 %collective-permute-done.3 = f32[4,384,256]{2,1,0:T(8,128)S(1)} collective-permute-done((f32[4,384,256]{2,1,0:T(8,128)S(1)}, f32[4,384,256]{2,1,0:T(8,128)S(1)}, u32[]{:S(2)}, u32[]{:S(2)}) %collective-permute-start.3) | collective-permute-done | bytes 1572896 | tf_op jit(solution)/shard_map/ppermute | solution.py:16
  231.7 0.2 fusion.75
  231.9 1.3 collective-permute-start.4
  233.2 0.7 fusion.39
  233.9 36.2 %collective-permute-done.4 = f32[4,384,256]{2,1,0:T(8,128)S(1)} collective-permute-done((f32[4,384,256]{2,1,0:T(8,128)S(1)}, f32[4,384,256]{2,1,0:T(8,128)S(1)}, u32[]{:S(2)}, u32[]{:S(2)}) %collective-permute-start.4) | collective-permute-done | bytes 1572896 | tf_op jit(solution)/shard_map/ppermute | solution.py:16
  270.1 1.3 fusion.74
  271.5 1.3 collective-permute-start.5
  272.8 0.8 fusion.40
  273.5 0.7 fusion.41
  274.3 68.8 %psum.7 = f32[]{:T(128)} all-reduce(f32[]{:T(128)} %get-tuple-element.79), channel_id=1, replica_groups=mesh['layer'=4,'latent'=8] {'layer','latent'}, use_global_device_ids=true, to_apply=%region_22.24 | all-reduce | flops 1 | bytes 8 | tf_op jit(solution)/shard_map/psum | solution.py:75
  343.7 0.7 fusion.8
  344.4 0.7 copy-done.3
  345.1 0.7 fusion.7
  345.7 0.7 copy-done.5
  346.4 0.7 fusion.6
  347.1 0.7 copy-done.7
  347.7 0.7 fusion.5
  348.4 2.1 maximum_bitcast_fusion
  350.5 1.3 fusion.76
  351.8 1.6 fusion.9
  353.4 0.6 broadcast_multiply_fusion
  (114 shorter events, 3.9 us)
Async XLA Ops:
  7.2 34.6 %copy-start = (bf16[1,1792,256]{2,1,0:T(8,128)(2,1)S(1)}, bf16[1,1792,256]{2,1,0:T(8,128)(2,1)}, u32[]{:S(2)}) copy-start(bf16[1,1792,256]{2,1,0:T(8,128)(2,1)} %param.18) | copy-start | bytes 2752516
  7.2 32.1 %all-gather.6.cloned.1.call-start = ((), (), s32[]{:S(2)}) async-start(), calls=%async_computation.3 | async-start | bytes 2064384 | tf_op jit(solution)/shard_map/all_gather | solution.py:39
  7.9 137.3 %reduce-scatter.2.cloned.1.call-start = ((), (), s32[]{:S(2)}) async-start(), calls=%async_computation.1 | async-start | bytes 4128768 | tf_op jit(solution)/shard_map/reduce_scatter | solution.py:71
  41.5 0.7 copy-start.27
  41.7 2.4 copy-start.13
  44.1 16.8 %collective-permute-start = (bf16[384,256]{1,0:T(8,128)(2,1)S(1)}, bf16[384,256]{1,0:T(8,128)(2,1)S(1)}, u32[]{:S(2)}, u32[]{:S(2)}) collective-permute-start(bf16[384,256]{1,0:T(8,128)(2,1)S(1)} %get-tuple-element.75), channel_id=1, source_target_pairs={{0,8},{8,16},{16,24},{1,9},{9,17},{17,25},{2,10},{10,18},{18,26},{... | collective-permute-start | bytes 589832 | tf_op jit(solution)/shard_map/ppermute | solution.py:16
  60.9 6.8 %copy-start.17 = (bf16[384,256]{1,0:T(8,128)(2,1)}, bf16[384,256]{1,0:T(8,128)(2,1)S(1)}, u32[]{:S(2)}) copy-start(bf16[384,256]{1,0:T(8,128)(2,1)S(1)} %collective-permute-done) | copy-start | bytes 589828
  60.9 14.8 %collective-permute-start.1 = (bf16[384,256]{1,0:T(8,128)(2,1)S(1)}, bf16[384,256]{1,0:T(8,128)(2,1)S(1)}, u32[]{:S(2)}, u32[]{:S(2)}) collective-permute-start(bf16[384,256]{1,0:T(8,128)(2,1)S(1)} %collective-permute-done), channel_id=1, source_target_pairs={{0,8},{8,16},{16,24},{1,9},{9,17},{17,25},{2,10},{10,18},{18,26},{... | collective-permute-start | bytes 589832 | tf_op jit(solution)/shard_map/ppermute | solution.py:16
  75.7 6.5 %copy-start.15 = (bf16[384,256]{1,0:T(8,128)(2,1)}, bf16[384,256]{1,0:T(8,128)(2,1)S(1)}, u32[]{:S(2)}) copy-start(bf16[384,256]{1,0:T(8,128)(2,1)S(1)} %collective-permute-done.1) | copy-start | bytes 589828
  75.7 14.5 %collective-permute-start.2 = (bf16[384,256]{1,0:T(8,128)(2,1)S(1)}, bf16[384,256]{1,0:T(8,128)(2,1)S(1)}, u32[]{:S(2)}, u32[]{:S(2)}) collective-permute-start(bf16[384,256]{1,0:T(8,128)(2,1)S(1)} %collective-permute-done.1), channel_id=1, source_target_pairs={{0,8},{8,16},{16,24},{1,9},{9,17},{17,25},{2,10},{10,18},{18,26},{... | collective-permute-start | bytes 589832 | tf_op jit(solution)/shard_map/ppermute | solution.py:16
  90.3 3.4 copy-start.19
  101.7 43.5 %copy-start.22 = (bf16[1,64,1792]{2,1,0:T(8,128)(2,1)S(1)}, bf16[1,64,1792]{2,1,0:T(8,128)(2,1)}, u32[]{:S(2)}) copy-start(bf16[1,64,1792]{2,1,0:T(8,128)(2,1)} %param.17) | copy-start | bytes 688132
  101.7 71.4 %all-gather.4.cloned.1.call-start = ((), (), s32[]{:S(2)}) async-start(), calls=%async_computation.2 | async-start | bytes 2064384 | tf_op jit(solution)/shard_map/all_gather | solution.py:77
  173.1 3.4 copy-start.1
  180.0 2.0 copy-start.26
  183.6 1.9 copy-start.10
  183.6 1.9 copy-start.25
  185.5 1.3 copy-start.9
  185.5 1.3 copy-start.24
  185.5 1.5 copy-start.23
  186.8 3.9 %copy-start.2 = (bf16[6,64,1792]{2,1,0:T(8,128)(2,1)}, bf16[6,64,1792]{2,1,0:T(8,128)(2,1)S(1)}, u32[]{:S(2)}) copy-start(bf16[6,64,1792]{2,1,0:T(8,128)(2,1)S(1)} %broadcast_select_fusion.2) | copy-start | bytes 4128772
  186.8 1.8 copy-start.8
  186.8 3.3 copy-start.11
  188.7 2.1 copy-start.4
  188.9 2.4 copy-start.6
  192.0 1.2 copy-start.12
  193.1 40.1 %copy-start.18 = (bf16[384,256]{1,0:T(8,128)(2,1)S(1)}, bf16[384,256]{1,0:T(8,128)(2,1)}, u32[]{:S(2)}) copy-start(bf16[384,256]{1,0:T(8,128)(2,1)} %copy-done.17) | copy-start | bytes 589828
  193.1 38.5 %collective-permute-start.3 = (f32[4,384,256]{2,1,0:T(8,128)S(1)}, f32[4,384,256]{2,1,0:T(8,128)S(1)}, u32[]{:S(2)}, u32[]{:S(2)}) collective-permute-start(f32[4,384,256]{2,1,0:T(8,128)S(1)} %pad_maximum_fusion), channel_id=1, source_target_pairs={{8,0},{16,8},{24,16},{9,1},{17,9},{25,17},{10,2},{18,10},{26,18},{... | collective-permute-start | bytes 4718600 | tf_op jit(solution)/shard_map/ppermute | solution.py:16
  231.9 38.2 %collective-permute-start.4 = (f32[4,384,256]{2,1,0:T(8,128)S(1)}, f32[4,384,256]{2,1,0:T(8,128)S(1)}, u32[]{:S(2)}, u32[]{:S(2)}) collective-permute-start(f32[4,384,256]{2,1,0:T(8,128)S(1)} %fusion.75), channel_id=1, source_target_pairs={{8,0},{16,8},{24,16},{9,1},{17,9},{25,17},{10,2},{18,10},{26,18},{... | collective-permute-start | bytes 4718600 | tf_op jit(solution)/shard_map/ppermute | solution.py:16
  233.9 38.9 %copy-start.16 = (bf16[384,256]{1,0:T(8,128)(2,1)S(1)}, bf16[384,256]{1,0:T(8,128)(2,1)}, u32[]{:S(2)}) copy-start(bf16[384,256]{1,0:T(8,128)(2,1)} %copy-done.15) | copy-start | bytes 589828
  233.9 39.6 %copy-start.20 = (bf16[384,256]{1,0:T(8,128)(2,1)S(1)}, bf16[384,256]{1,0:T(8,128)(2,1)}, u32[]{:S(2)}) copy-start(bf16[384,256]{1,0:T(8,128)(2,1)} %copy-done.19) | copy-start | bytes 589828
  271.5 79.0 %collective-permute-start.5 = (f32[4,384,256]{2,1,0:T(8,128)}, f32[4,384,256]{2,1,0:T(8,128)}, u32[]{:S(2)}, u32[]{:S(2)}) collective-permute-start(f32[4,384,256]{2,1,0:T(8,128)} %fusion.74), channel_id=1, source_target_pairs={{8,0},{16,8},{24,16},{9,1},{17,9},{25,17},{10,2},{18,10},{26,18},{... | collective-permute-start | bytes 4718600 | tf_op jit(solution)/shard_map/ppermute | solution.py:16
  343.7 1.3 copy-start.3
  345.1 1.3 copy-start.5
  346.4 1.3 copy-start.7
  348.4 2.1 copy-start.21
  348.4 3.4 copy-start.14
Sparse Core Ops, SparseCore 0:
  9.7 29.6 all-gather.5
  101.8 43.3 reduce-scatter.1
  147.8 25.2 all-gather.3
where the time goes:
time: 363 us; the launch traced here: 362 us
  waiting for transfers between devices  166 us (46%)
  blocking collectives  68.8 us (19%)
  other arithmetic  52.7 us (15%)
  matrix products  22.8 us (6%)
  local copies, waits for them, and re-layouts  21.1 us (6%)
  between operations  16.1 us (4%)
  starting transfers between devices  14.2 us (4%)
    ppermute x6, waiting for transfers between devices, shifted(): lax.ppermute(value, axis, [(source, source + steps) for source in range(l...  73.3 us
    psum x1, blocking collectives, shards(): total = lax.psum(jnp.sum(errors * errors), ('layer', 'latent'))  68.8 us
    reduce_scatter x1, waiting for transfers between devices, shards(): lax.psum_scatter(writes.reshape(NTILE * TILE, D), 'latent', scatter_dimen...  43.2 us
    scatter-add x4, other arithmetic, take_source(): writes = writes.at[tile_ids].add(product)  32 us
    all_gather x1, waiting for transfers between devices, shards(): lax.all_gather(residual[0], 'latent', axis=0, tiled=True)  27 us
    all_gather x1, waiting for transfers between devices, shards(): lax.all_gather(errors.astype(jnp.bfloat16), 'latent', axis=0, tiled=True)  21.6 us
    ppermute x6, starting transfers between devices, shifted(): lax.ppermute(value, axis, [(source, source + steps) for source in range(l...  14.1 us
    dot_general x4, matrix products, take_source(): jnp.dot(portion, weight, preferred_element_type=jnp.float32)  13.2 us
  transfers between devices with their start and end apart: 9, of which 5 were waited for; matrix products, arithmetic and copies ran while one was open for 14% of the time, Pallas kernels for 0%

commit v1 on v0

--- a/solution.py
+++ b/solution.py
@@ -1,6 +1,10 @@
+import functools
+
 import jax
 import jax.numpy as jnp
 from jax import lax
+from jax.experimental import pallas as pl
+from jax.experimental.pallas import tpu as pltpu
 from jax.sharding import PartitionSpec as P
 
 D = 1792
@@ -8,6 +12,370 @@
 TILE = 64
 NTILE = 8
 CAP = 6
+CHIPS = NTILE // 2
+PAIR = 2 * TILE
+TOKENS = NTILE * TILE
+LAYERS = 4
+CHUNKS = 2
+CW = D // CHUNKS
+MESH = pl.DeviceIdType.MESH
+ORDER = (1, 3, 2)
+
+
+def fused_kernel(
+    res, tgt, enc_w, bias, dec_w, active,
+    loss, enc_g, bias_g, dec_g,
+    x, xt, we, wd, goal, masked, codes, part, part_in, shares, share_in, err,
+    grad, grad_bf, grad_in, dec_v, enc_v, acc, sum_core, sum_chip, sum_layer,
+    load_sem, store_sem, x_send, x_recv, xp_send, xp_recv, c_send, c_recv,
+    p_send, p_recv, s_send, s_recv, e_send, e_recv, ep_send, ep_recv, g_send, g_recv,
+    l_send, l_recv,
+):
+    layer = lax.axis_index("layer")
+    latent = lax.axis_index("latent")
+    z = latent // 2
+    core = latent % 2
+    partner = (layer, 2 * z + 1 - core)
+
+    def chip(k):
+        return (layer, 2 * lax.rem(z + k, CHIPS) + core)
+
+    def half(slot):
+        return pl.ds(pl.multiple_of(slot * PAIR + core * TILE, TILE), TILE)
+
+    def remote(src, dst, send, recv, device):
+        return pltpu.make_async_remote_copy(
+            src_ref=src, dst_ref=dst, send_sem=send, recv_sem=recv,
+            device_id=device, device_id_type=MESH,
+        )
+
+    own_cols = pl.ds(pl.multiple_of(layer * BLOCK, BLOCK), BLOCK)
+    loads = [
+        pltpu.make_async_copy(res.at[0], x.at[half(0)], load_sem.at[0]),
+        pltpu.make_async_copy(enc_w.at[0], we, load_sem.at[1]),
+        pltpu.make_async_copy(dec_w.at[:, 0], wd, load_sem.at[2]),
+        pltpu.make_async_copy(tgt.at[0], goal, load_sem.at[3]),
+    ]
+    for load in loads:
+        load.start()
+
+    barrier = pltpu.get_barrier_semaphore()
+    pl.semaphore_signal(barrier, inc=1, device_id=partner, device_id_type=MESH)
+    for k in range(1, CHIPS):
+        pl.semaphore_signal(barrier, inc=1, device_id=chip(k), device_id_type=MESH)
+    for d in range(1, LAYERS):
+        pl.semaphore_signal(
+            barrier, inc=1, device_id=(lax.rem(layer + d, LAYERS), latent), device_id_type=MESH
+        )
+    pl.semaphore_wait(barrier, 1 + CHIPS - 1 + LAYERS - 1)
+
+    x_out = {
+        k: remote(res.at[0], x.at[half(k)], x_send.at[k], x_recv.at[k], chip(k)) for k in ORDER
+    }
+    xp_out = {0: remote(res.at[0], x.at[half(0)], xp_send.at[0], xp_recv.at[0], partner)}
+    xp_out[0].start()
+    for k in ORDER:
+        x_out[k].start()
+
+    for s in range(1, LAYERS):
+        @pl.when(s > layer)
+        def _(s=s):
+            codes[:, s * BLOCK:(s + 1) * BLOCK] = jnp.zeros((TOKENS, BLOCK), jnp.bfloat16)
+
+    def code_copy(q, t):
+        block = codes.at[pl.ds(q * PAIR, PAIR), own_cols]
+        return remote(block, block, c_send.at[t, q], c_recv.at[layer, q], (t, latent))
+
+    def code_wait(q, s):
+        block = codes.at[pl.ds(q * PAIR, PAIR), pl.ds(s * BLOCK, BLOCK)]
+        return remote(block, block, c_send.at[s, q], c_recv.at[s, q], (s, latent))
+
+    def encode(q):
+        rows = pl.ds(q * PAIR, PAIR)
+        pre = jnp.dot(x[rows, :], we[...], preferred_element_type=jnp.float32) + bias[...]
+        first = 2 * lax.rem(z + CHIPS - q, CHIPS)
+        for c in range(2):
+            listed = [active[layer, first + c, a] for a in range(active.shape[2])]
+            hit = functools.reduce(jnp.logical_or, [b == latent for b in listed])
+            live = jnp.where(hit, 1.0, 0.0).astype(jnp.float32)
+            kept = pre[c * TILE:(c + 1) * TILE] * live
+            spot = pl.ds(q * PAIR + c * TILE, TILE)
+            masked[spot, :] = kept
+            codes[spot, own_cols] = jnp.maximum(kept, 0.0).astype(jnp.bfloat16)
+        for t in range(1, LAYERS):
+            @pl.when(t > layer)
+            def _(t=t):
+                code_copy(q, t).start()
+
+    def take_x(k):
+        x_out[k].wait_recv()
+        xp_out[k] = remote(x.at[half(k)], x.at[half(k)], xp_send.at[k], xp_recv.at[k], partner)
+        xp_out[k].start()
+
+    loads[0].wait()
+    loads[1].wait()
+    xp_out[0].wait_recv()
+    encode(0)
+    take_x(1)
+    take_x(3)
+    xp_out[1].wait_recv()
+    encode(1)
+    take_x(2)
+    xp_out[3].wait_recv()
+    encode(3)
+    xp_out[2].wait_recv()
+    encode(2)
+
+    loads[2].wait()
+    for q in range(CHIPS):
+        for s in range(LAYERS - 1):
+            @pl.when(s < layer)
+            def _(q=q, s=s):
+                code_wait(q, s).wait_recv()
+    p_out = []
+    for j in range(CHUNKS):
+        cols = slice(j * CW, (j + 1) * CW)
+        full = jnp.dot(
+            codes[...], wd[:, :, cols].reshape(LAYERS * BLOCK, CW),
+            preferred_element_type=jnp.float32,
+        ).astype(jnp.bfloat16)
+        for q in range(CHIPS):
+            for c in range(2):
+                at = q * PAIR + c * TILE
+                part[j, c, q] = full[at:at + TILE]
+        p_out.append(
+            remote(part.at[j, 1 - core], part_in.at[j], p_send.at[j], p_recv.at[j], partner)
+        )
+        p_out[j].start()
+    s_out = {}
+    for j in range(CHUNKS):
+        p_out[j].wait_recv()
+        for k in ORDER:
+            own = part[j, core, CHIPS - k].astype(jnp.float32)
+            other = part_in[j, CHIPS - k].astype(jnp.float32)
+            shares[j, k] = (own + other).astype(jnp.bfloat16)
+            s_out[j, k] = remote(
+                shares.at[j, k], share_in.at[j, k], s_send.at[j, k], s_recv.at[j, k], chip(k)
+            )
+            s_out[j, k].start()
+
+    xt[...] = x[...].T
+
+    loads[3].wait()
+    e_out, ep_out = {}, {}
+    squares = jnp.zeros((8, 128), jnp.float32)
+    for j in range(CHUNKS):
+        cols = pl.ds(j * CW, CW)
+        total = part[j, core, 0].astype(jnp.float32) + part_in[j, 0].astype(jnp.float32)
+        for k in ORDER:
+            s_out[j, k].wait_recv()
+            total = total + share_in[j, k].astype(jnp.float32)
+        error = total - goal[:, j * CW:(j + 1) * CW].astype(jnp.float32)
+        err[half(0), cols] = error.astype(jnp.bfloat16)
+        block = err.at[half(0), cols]
+        for k in ORDER:
+            e_out[j, k] = remote(
+                block, err.at[half(k), cols], e_send.at[j, k], e_recv.at[j, k], chip(k)
+            )
+            e_out[j, k].start()
+        ep_out[j, 0] = remote(block, block, ep_send.at[j, 0], ep_recv.at[j, 0], partner)
+        ep_out[j, 0].start()
+        square = jnp.sum((error * error).reshape(TILE // 8, 8, CW), axis=0)
+        for b in range(CW // 128):
+            squares = squares + square[:, b * 128:(b + 1) * 128]
+
+    sum_core[core] = squares
+    l_core = remote(sum_core.at[core], sum_core.at[core], l_send.at[0], l_recv.at[0], partner)
+    l_core.start()
+    l_core.wait_recv()
+    sum_chip[z] = sum_core[0] + sum_core[1]
+    l_chip = [
+        remote(sum_chip.at[z], sum_chip.at[z], l_send.at[k], l_recv.at[k], chip(k))
+        for k in range(1, CHIPS)
+    ]
+    for copy in l_chip:
+        copy.start()
+
+    def take_e(k):
+        for j in range(CHUNKS):
+            e_out[j, k].wait_recv()
+            block = err.at[half(k), pl.ds(j * CW, CW)]
+            ep_out[j, k] = remote(block, block, ep_send.at[j, k], ep_recv.at[j, k], partner)
+            ep_out[j, k].start()
+
+    def grad_copy(h, s):
+        rows = pl.ds(h * 2 * PAIR, 2 * PAIR)
+        return remote(
+            grad_bf.at[rows, pl.ds(s * BLOCK, BLOCK)], grad_in.at[layer, rows],
+            g_send.at[s, h], g_recv.at[layer, h], (s, latent),
+        )
+
+    def grad_wait(h, t):
+        rows = pl.ds(h * 2 * PAIR, 2 * PAIR)
+        return remote(
+            grad_bf.at[rows, pl.ds(0, BLOCK)], grad_in.at[t, rows],
+            g_send.at[t, h], g_recv.at[t, h], (t, latent),
+        )
+
+    def code_grad(h):
+        rows = pl.ds(h * 2 * PAIR, 2 * PAIR)
+        back = lax.dot_general(
+            err[rows, :], wd[...].reshape(LAYERS * BLOCK, D),
+            (((1,), (1,)), ((), ())), preferred_element_type=jnp.float32,
+        )
+        grad[rows, :] = back
+        grad_bf[rows, :] = back.astype(jnp.bfloat16)
+        for s in range(LAYERS - 1):
+            @pl.when(s < layer)
+            def _(s=s):
+                grad_copy(h, s).start()
+
+    take_e(1)
+    for copy in l_chip:
+        copy.wait_recv()
+    sum_layer[layer] = functools.reduce(jnp.add, [sum_chip[i] for i in range(CHIPS)])
+    l_layer = [
+        remote(
+            sum_layer.at[layer], sum_layer.at[layer],
+            l_send.at[CHIPS - 1 + d], l_recv.at[CHIPS - 1 + d],
+            (lax.rem(layer + d, LAYERS), latent),
+        )
+        for d in range(1, LAYERS)
+    ]
+    for copy in l_layer:
+        copy.start()
+    take_e(3)
+    for k in (0, 1):
+        for j in range(CHUNKS):
+            ep_out[j, k].wait_recv()
+    code_grad(0)
+    take_e(2)
+    for k in (3, 2):
+        for j in range(CHUNKS):
+            ep_out[j, k].wait_recv()
+    code_grad(1)
+
+    stores = []
+    for s in range(LAYERS):
+        dec_v[s] = (
+            lax.dot_general(
+                codes[:, s * BLOCK:(s + 1) * BLOCK], err[...],
+                (((0,), (0,)), ((), ())), preferred_element_type=jnp.float32,
+            ) * (1.0 / TILE)
+        ).astype(jnp.bfloat16)
+        stores.append(pltpu.make_async_copy(dec_v.at[s], dec_g.at[s, 0], store_sem.at[s]))
+        stores[s].start()
+
+    acc[...] = grad[:, own_cols]
+    for t in range(1, LAYERS):
+        @pl.when(t > layer)
+        def _(t=t):
+            grad_wait(0, t).wait_recv()
+            grad_wait(1, t).wait_recv()
+            acc[...] += grad_in[t].astype(jnp.float32)
+    pre_grad = jnp.where(masked[...] > 0, acc[...], 0.0)
+    bias_g[...] = jnp.sum(pre_grad, axis=0, keepdims=True) * (1.0 / TILE)
+    enc_v[...] = (
+        jnp.dot(xt[...], pre_grad.astype(jnp.bfloat16), preferred_element_type=jnp.float32)
+        * (1.0 / TILE)
+    ).astype(jnp.bfloat16)
+    stores.append(pltpu.make_async_copy(enc_v, enc_g.at[0], store_sem.at[LAYERS]))
+    stores[LAYERS].start()
+
+    for copy in l_layer:
+        copy.wait_recv()
+    every = functools.reduce(jnp.add, [sum_layer[i] for i in range(LAYERS)])
+    loss[...] = jnp.sum(every, keepdims=True) * (0.5 / (LAYERS * TOKENS * D))
+
+    for copies in (x_out, xp_out, s_out, e_out, ep_out):
+        for copy in copies.values():
+            copy.wait_send()
+    for copy in [*p_out, l_core, *l_chip, *l_layer]:
+        copy.wait_send()
+    for t in range(LAYERS):
+        @pl.when(t > layer)
+        def _(t=t):
+            for q in range(CHIPS):
+                code_copy(q, t).wait_send()
+
+        @pl.when(t < layer)
+        def _(t=t):
+            for h in range(2):
+                grad_copy(h, t).wait_send()
+    for store in stores:
+        store.wait()
+
+
+def fused(residual, target, enc_weight, enc_bias, dec_weight, active):
+    bf, f32 = jnp.bfloat16, jnp.float32
+    vmem, dma = pltpu.VMEM, pltpu.SemaphoreType.DMA
+    anywhere = pl.BlockSpec(memory_space=pl.ANY)
+    in_vmem = pl.BlockSpec(memory_space=pltpu.VMEM)
+    loss, enc_grad, bias_grad, dec_grad = pl.pallas_call(
+        fused_kernel,
+        out_shape=[
+            jax.ShapeDtypeStruct((1, 1), f32),
+            jax.ShapeDtypeStruct(enc_weight.shape, bf),
+            jax.ShapeDtypeStruct(enc_bias.shape, f32),
+            jax.ShapeDtypeStruct(dec_weight.shape, bf),
+        ],
+        in_specs=[
+            anywhere, anywhere, anywhere, in_vmem, anywhere,
+            pl.BlockSpec(memory_space=pltpu.SMEM),
+        ],
+        out_specs=[in_vmem, anywhere, in_vmem, anywhere],
+        scratch_shapes=[
+            vmem((TOKENS, D), bf),
+            vmem((D, TOKENS), bf),
+            vmem((D, BLOCK), bf),
+            vmem((LAYERS, BLOCK, D), bf),
+            vmem((TILE, D), bf),
+            vmem((TOKENS, BLOCK), f32),
+            vmem((TOKENS, LAYERS * BLOCK), bf),
+            vmem((CHUNKS, 2, CHIPS, TILE, CW), bf),
+            vmem((CHUNKS, CHIPS, TILE, CW), bf),
+            vmem((CHUNKS, CHIPS, TILE, CW), bf),
+            vmem((CHUNKS, CHIPS, TILE, CW), bf),
+            vmem((TOKENS, D), bf),
+            vmem((TOKENS, LAYERS * BLOCK), f32),
+            vmem((TOKENS, LAYERS * BLOCK), bf),
+            vmem((LAYERS, TOKENS, BLOCK), bf),
+            vmem((LAYERS, BLOCK, D), bf),
+            vmem((D, BLOCK), bf),
+            vmem((TOKENS, BLOCK), f32),
+            vmem((2, 8, 128), f32),
+            vmem((CHIPS, 8, 128), f32),
+            vmem((LAYERS, 8, 128), f32),
+            dma((4,)),
+            dma((LAYERS + 1,)),
+            dma((CHIPS,)),
+            dma((CHIPS,)),
+            dma((CHIPS,)),
+            dma((CHIPS,)),
+            dma((LAYERS, CHIPS)),
+            dma((LAYERS, CHIPS)),
+            dma((CHUNKS,)),
+            dma((CHUNKS,)),
+            dma((CHUNKS, CHIPS)),
+            dma((CHUNKS, CHIPS)),
+            dma((CHUNKS, CHIPS)),
+            dma((CHUNKS, CHIPS)),
+            dma((CHUNKS, CHIPS)),
+            dma((CHUNKS, CHIPS)),
+            dma((LAYERS, 2)),
+            dma((LAYERS, 2)),
+            dma((CHIPS + LAYERS - 1,)),
+            dma((CHIPS + LAYERS - 1,)),
+        ],
+        compiler_params=pltpu.CompilerParams(
+            collective_id=0, has_side_effects=True, vmem_limit_bytes=48 * 2**20
+        ),
+        cost_estimate=pl.CostEstimate(
+            flops=14 * 2 * TOKENS * D * BLOCK, bytes_accessed=10 * 2**20, transcendentals=0
+        ),
+        name="transcoder_step",
+    )(residual, target, enc_weight, enc_bias, dec_weight, active)
+    return (loss[0, 0], enc_grad, bias_grad, dec_grad)
 
 
 def shifted(value, axis, steps):
@@ -126,4 +494,6 @@
         P("layer", "latent"),
         P(None, "layer", "latent", None),
     )
-    return jax.shard_map(shards, mesh=mesh, in_specs=in_specs, out_specs=out_specs, check_vma=False)
+    one_tile_each = mesh.shape["latent"] == NTILE and mesh.shape["layer"] == LAYERS
+    step = fused if one_tile_each else shards
+    return jax.shard_map(step, mesh=mesh, in_specs=in_specs, out_specs=out_specs, check_vma=False)

time: 363 us -> 111 us (0.31)
  waiting for transfers between devices: 166 us -> 0 us
  Pallas kernels: 0 us -> 96 us
  blocking collectives: 68.8 us -> 0 us
  other arithmetic: 52.7 us -> 0 us
  matrix products: 22.8 us -> 0 us
  starting transfers between devices: 14.2 us -> 0 us
  between operations: 16.1 us -> 2.33 us
  local copies, waits for them, and re-layouts: 21.1 us -> 11.9 us
    pallas_call x0 -> x1, Pallas kernels: none -> 96 us  [fused(): pl.pallas_call(fused_kernel, out_shape=[jax.ShapeDtypeStruct((1, 1), f32)...]
    ppermute x6 -> x0, waiting for transfers between devices: 73.3 us -> none  [shifted(): lax.ppermute(value, axis, [(source, source + steps) for source in range(l...]
    psum x1 -> x0, blocking collectives: 68.8 us -> none  [shards(): total = lax.psum(jnp.sum(errors * errors), ('layer', 'latent'))]
    all_gather x2 -> x0, waiting for transfers between devices: 48.6 us -> none  [the longest x1 27 us: shards(): lax.all_gather(residual[0], 'latent', axis=0, tiled=True)]
    reduce_scatter x1 -> x0, waiting for transfers between devices: 43.2 us -> none  [shards(): lax.psum_scatter(writes.reshape(NTILE * TILE, D), 'latent', scatter_dimen...]
    scatter-add x4 -> x0, other arithmetic: 32 us -> none  [take_source(): writes = writes.at[tile_ids].add(product)]
    dot_general x14 -> x0, matrix products: 22.8 us -> none  [the longest x4 13.2 us: take_source(): jnp.dot(portion, weight, preferred_element_type=jnp.float32)]
    ppermute x6 -> x0, starting transfers between devices: 14.1 us -> none  [shifted(): lax.ppermute(value, axis, [(source, source + steps) for source in range(l...]
  transfers between devices with their start and end apart: 9 -> 0, of which waited for: 5 -> 0; matrix products, arithmetic and copies ran while one was open for 14% -> 0% of each run, Pallas kernels for 0% -> 0%
where the time goes in v1:
time: 111 us; the launch traced here: 110 us
  Pallas kernels  96 us (86%)
  local copies, waits for them, and re-layouts  11.9 us (11%)
  between operations  2.33 us (2%)
    pallas_call x1, Pallas kernels, fused(): pl.pallas_call(fused_kernel, out_shape=[jax.ShapeDtypeStruct((1, 1), f32)...  96 us
    unnamed x14, local copies, waits for them, and re-layouts  11.9 us

profile of v1, /device:TPU:0, one launch (start us, length us, event | category | flops | bytes accessed | tf_op | source)
XLA Modules:
  0.0 110.3 jit_solution(5310650790529562245)
XLA Ops:
  0.6 0.8 copy.10.active
  1.4 0.0 copy-start.1
  1.4 1.2 %copy-done.1 = bf16[1,1792,256]{2,1,0:T(8,128)(2,1)S(1)} copy-done((bf16[1,1792,256]{2,1,0:T(8,128)(2,1)S(1)}, bf16[1,1792,256]{2,1,0:T(8,128)(2,1)}, u32[]{:S(2)}) %copy-start.1) | copy-done | bytes 917528
  2.6 0.0 copy-start.2
  2.6 0.9 copy-done.2
  3.5 0.0 copy-start.3
  3.5 0.9 copy-done.3
  4.5 0.0 copy-start.4
  4.5 0.7 copy-done.4
  5.2 96.0 %transcoder_step.1 = (f32[1,1]{1,0:T(1,128)}, bf16[1,1792,256]{2,1,0:T(8,128)(2,1)S(1)}, f32[1,256]{1,0:T(1,128)S(1)}, bf16[4,1,256,1792]{3,2,1,0:T(8,128)(2,1)S(1)}) custom-call(bf16[1,64,1792]{2,1,0:T(8,128)(2,1)S(1)} %copy-done.2, bf16[1,64,1792]{2,1,0:T(8,128)(2,1)S(1)} %copy-done.3, bf16[1,1792,256]{2,1,0:T(8,128)(2,1)S(1)} %copy-done.1, ...), custom_call_target="tpu_custom_call" | custom-call | flops 6576668672 | bytes 10485760 | tf_op jit(solution)/shard_map/transcoder_step/pallas_call | solution.py:314
  101.2 0.0 copy-start
  101.2 1.8 %copy-done = bf16[4,1,256,1792]{3,2,1,0:T(8,128)(2,1)} copy-done((bf16[4,1,256,1792]{3,2,1,0:T(8,128)(2,1)}, bf16[4,1,256,1792]{3,2,1,0:T(8,128)(2,1)S(1)}, u32[]{:S(2)}) %copy-start) | copy-done | bytes 3670040
  103.5 0.9 copy.16
  104.5 0.6 copy.17
  105.0 4.1 %copy.18 = bf16[4,1,256,1792]{3,2,1,0:T(8,128)(2,1)} copy(bf16[4,1,256,1792]{3,2,1,0:T(8,128)(2,1)} %copy-done) | data formatting | bytes 7340032
Async XLA Ops:
  1.4 1.2 %copy-start.1 = (bf16[1,1792,256]{2,1,0:T(8,128)(2,1)S(1)}, bf16[1,1792,256]{2,1,0:T(8,128)(2,1)}, u32[]{:S(2)}) copy-start(bf16[1,1792,256]{2,1,0:T(8,128)(2,1)} %enc_w.1) | copy-start | bytes 2752516
  2.6 0.9 copy-start.2
  3.5 0.9 copy-start.3
  4.5 0.7 copy-start.4
  101.2 1.8 %copy-start = (bf16[4,1,256,1792]{3,2,1,0:T(8,128)(2,1)}, bf16[4,1,256,1792]{3,2,1,0:T(8,128)(2,1)S(1)}, u32[]{:S(2)}) copy-start(bf16[4,1,256,1792]{3,2,1,0:T(8,128)(2,1)S(1)} %get-tuple-element.19) | copy-start | bytes 11010052

commit v2 on v1

v2 whole, which is shorter than its diff:
```python
import functools

import jax
import jax.numpy as jnp
from jax import lax
from jax.experimental import pallas as pl
from jax.experimental.pallas import tpu as pltpu
from jax.sharding import PartitionSpec as P

D = 1792
BLOCK = 256
TILE = 64
NTILE = 8
CAP = 6
CHIPS = NTILE // 2
PAIR = 2 * TILE
TOKENS = NTILE * TILE
LAYERS = 4
CHUNKS = 2
CW = D // CHUNKS
MESH = pl.DeviceIdType.MESH
GROUPS = ((0, 2 * PAIR), (2 * PAIR, PAIR), (3 * PAIR, PAIR))


def fused_kernel(
    res, tgt, enc_w, bias, dec_w, active,
    loss, enc_g, bias_g, dec_g,
    x, xt, we, wd, goal, offset, masked, codes, part, part_in, shares, share_in, err,
    grad, grad_bf, grad_in, acc, sum_core, sum_chip, sum_layer,
    load_sem, x_send, x_recv, xp_send, xp_recv, c_send, c_recv,
    p_send, p_recv, s_send, s_recv, e_send, e_recv, ep_send, ep_recv, g_send, g_recv,
    l_send, l_recv,
):
    layer = lax.axis_index("layer")
    latent = lax.axis_index("latent")
    z = latent // 2
    core = latent % 2
    middle = (z * (CHIPS - 1 - z)) // 2
    mates = (z, z + 1 - 2 * (z % 2), (z + 2) % CHIPS, CHIPS - 1 - z)
    partner = (layer, 2 * z + 1 - core)

    def chip(m):
        return (layer, 2 * mates[m] + core)

    def half(slot):
        return pl.ds(pl.multiple_of(slot * PAIR + core * TILE, TILE), TILE)

    def remote(src, dst, send, recv, device):
        return pltpu.make_async_remote_copy(
            src_ref=src, dst_ref=dst, send_sem=send, recv_sem=recv,
            device_id=device, device_id_type=MESH,
        )

    own_cols = pl.ds(pl.multiple_of(layer * BLOCK, BLOCK), BLOCK)
    loads = [
        pltpu.make_async_copy(res.at[0], x.at[half(0)], load_sem.at[0]),
        pltpu.make_async_copy(enc_w.at[0], we, load_sem.at[1]),
        pltpu.make_async_copy(bias, offset, load_sem.at[4]),
        pltpu.make_async_copy(dec_w.at[:, 0], wd, load_sem.at[2]),
        pltpu.make_async_copy(tgt.at[0], goal, load_sem.at[3]),
    ]
    for load in loads:
        load.start()

    barrier = pltpu.get_barrier_semaphore()
    pl.semaphore_signal(barrier, inc=1, device_id=partner, device_id_type=MESH)
    for m in range(1, CHIPS):
        pl.semaphore_signal(barrier, inc=1, device_id=chip(m), device_id_type=MESH)
    for d in range(1, LAYERS):
        pl.semaphore_signal(
            barrier, inc=1, device_id=(lax.rem(layer + d, LAYERS), latent), device_id_type=MESH
        )
    pl.semaphore_wait(barrier, 1 + CHIPS - 1 + LAYERS - 1)

    x_out = {
        m: remote(res.at[0], x.at[half(m)], x_send.at[m], x_recv.at[m], chip(m))
        for m in (1, 2, 3)
    }
    x_far = remote(x.at[half(2)], x.at[half(3)], x_send.at[0], x_recv.at[3], chip(1))
    xp_out = {0: remote(res.at[0], x.at[half(0)], xp_send.at[0], xp_recv.at[0], partner)}
    xp_out[0].start()
    for m in (1, 2):
        x_out[m].start()

    for s in range(1, LAYERS):
        @pl.when(s > layer)
        def _(s=s):
            codes[:, s * BLOCK:(s + 1) * BLOCK] = jnp.zeros((TOKENS, BLOCK), jnp.bfloat16)

    @pl.when(middle == 0)
    def _():
        for j in range(CHUNKS):
            share_in[j, 3] = jnp.zeros((TILE, CW), jnp.bfloat16)

    def code_copy(q, t):
        block = codes.at[pl.ds(q * PAIR, PAIR), own_cols]
        return remote(block, block, c_send.at[t, q], c_recv.at[layer, q], (t, latent))

    def code_wait(q):
        for s in range(LAYERS - 1):
            @pl.when(s < layer)
            def _(s=s):
                block = codes.at[pl.ds(q * PAIR, PAIR), pl.ds(s * BLOCK, BLOCK)]
                remote(
                    block, block, c_send.at[s, q], c_recv.at[s, q], (s, latent)
                ).wait_recv()

    def encode(q):
        rows = pl.ds(q * PAIR, PAIR)
        pre = jnp.dot(x[rows, :], we[...], preferred_element_type=jnp.float32) + offset[...]
        for c in range(2):
            listed = [active[layer, a, 2 * mates[q] + c] for a in range(active.shape[1])]
            hit = functools.reduce(jnp.logical_or, [b == latent for b in listed])
            live = jnp.where(hit, 1.0, 0.0).astype(jnp.float32)
            kept = pre[c * TILE:(c + 1) * TILE] * live
            spot = pl.ds(q * PAIR + c * TILE, TILE)
            masked[spot, :] = kept
            codes[spot, own_cols] = jnp.maximum(kept, 0.0).astype(jnp.bfloat16)
        for t in range(1, LAYERS):
            @pl.when(t > layer)
            def _(t=t):
                code_copy(q, t).start()

    def take_x(m):
        x_out[m].wait_recv()
        xp_out[m] = remote(x.at[half(m)], x.at[half(m)], xp_send.at[m], xp_recv.at[m], partner)
        xp_out[m].start()

    p_out, s_out = {}, {}

    def decode(g, j):
        full = jnp.dot(
            codes[g * 2 * PAIR:(g + 1) * 2 * PAIR, :],
            wd[:, :, j * CW:(j + 1) * CW].reshape(LAYERS * BLOCK, CW),
            preferred_element_type=jnp.float32,
        ).astype(jnp.bfloat16)
        for q in range(2):
            for c in range(2):
                at = q * PAIR + c * TILE
                part[g, j, c, q] = full[at:at + TILE]
        p_out[g, j] = remote(
            part.at[g, j, 1 - core], part_in.at[g, j], p_send.at[g, j], p_recv.at[g, j], partner
        )
        p_out[g, j].start()

    def chip_sum(j, m):
        own = part[m // 2, j, core, m % 2].astype(jnp.float32)
        return own + part_in[m // 2, j, m % 2].astype(jnp.float32)

    def send_share(j, m, slot, device):
        s_out[j, m] = remote(
            shares.at[j, m], share_in.at[j, slot], s_send.at[j, m], s_recv.at[j, slot], device
        )
        s_out[j, m].start()

    def share_wait(j, slot):
        remote(
            shares.at[j, slot], share_in.at[j, slot], s_send.at[j, slot], s_recv.at[j, slot],
            partner,
        ).wait_recv()

    loads[0].wait()
    loads[1].wait()
    loads[2].wait()
    xp_out[0].wait_recv()
    encode(0)
    take_x(1)
    take_x(2)

    @pl.when(middle == 1)
    def _():
        x_far.start()
        x_out[3].start()

    xp_out[1].wait_recv()
    encode(1)
    xp_out[2].wait_recv()
    encode(2)
    loads[3].wait()
    code_wait(0)
    code_wait(1)
    for j in range(CHUNKS):
        decode(0, j)
    take_x(3)
    for j in range(CHUNKS):
        p_out[0, j].wait_recv()
        shares[j, 1] = chip_sum(j, 1).astype(jnp.bfloat16)
        send_share(j, 1, 1, chip(1))
    xp_out[3].wait_recv()
    encode(3)
    code_wait(2)
    code_wait(3)
    for j in range(CHUNKS):
        decode(1, j)
    far = (layer, 2 * (middle * mates[3] + (1 - middle) * mates[1]) + core)
    for j in range(CHUNKS):
        p_out[1, j].wait_recv()
        shares[j, 3] = chip_sum(j, 3).astype(jnp.bfloat16)
        send_share(j, 3, 3 * middle, far)
    for j in range(CHUNKS):
        @pl.when(middle == 0)
        def _(j=j):
            shares[j, 2] = chip_sum(j, 2).astype(jnp.bfloat16)

        @pl.when(middle == 1)
        def _(j=j):
            share_wait(j, 0)
            shares[j, 2] = (
                chip_sum(j, 2) + share_in[j, 0].astype(jnp.float32)
            ).astype(jnp.bfloat16)

        send_share(j, 2, 2, chip(2))

    xt[...] = x[...].T

    loads[4].wait()
    e_out, ep_out, e_far = {}, {}, {}
    squares = jnp.zeros((8, 128), jnp.float32)
    for j in range(CHUNKS):
        cols = pl.ds(j * CW, CW)
        share_wait(j, 1)
        share_wait(j, 2)

        @pl.when(middle == 1)
        def _(j=j):
            share_wait(j, 3)

        total = chip_sum(j, 0)
        for m in (1, 2, 3):
            total = total + share_in[j, m].astype(jnp.float32)
        error = total - goal[:, j * CW:(j + 1) * CW].astype(jnp.float32)
        err[half(0), cols] = error.astype(jnp.bfloat16)
        block = err.at[half(0), cols]
        for m in (1, 2, 3):
            e_out[j, m] = remote(
                block, err.at[half(m), cols], e_send.at[j, m], e_recv.at[j, m], chip(m)
            )
        e_far[j] = remote(
            err.at[half(2), cols], err.at[half(3), cols], e_send.at[j, 0], e_recv.at[j, 3], chip(1)
        )
        for m in (2, 1):
            e_out[j, m].start()
        ep_out[j, 0] = remote(block, block, ep_send.at[j, 0], ep_recv.at[j, 0], partner)
        ep_out[j, 0].start()
        square = jnp.sum((error * error).reshape(TILE // 8, 8, CW), axis=0)
        for b in range(CW // 128):
            squares = squares + square[:, b * 128:(b + 1) * 128]

    sum_core[core] = squares
    l_core = remote(sum_core.at[core], sum_core.at[core], l_send.at[0], l_recv.at[0], partner)
    l_core.start()

    def take_e(j, m):
        e_out[j, m].wait_recv()
        block = err.at[half(m), pl.ds(j * CW, CW)]
        ep_out[j, m] = remote(block, block, ep_send.at[j, m], ep_recv.at[j, m], partner)
        ep_out[j, m].start()

    def grad_copy(i, s):
        rows = pl.ds(*GROUPS[i])
        return remote(
            grad_bf.at[rows, pl.ds(s * BLOCK, BLOCK)], grad_in.at[layer, rows],
            g_send.at[s, i], g_recv.at[layer, i], (s, latent),
        )

    def grad_wait(i, t):
        rows = pl.ds(*GROUPS[i])
        remote(
            grad_bf.at[rows, pl.ds(0, BLOCK)], grad_in.at[t, rows],
            g_send.at[t, i], g_recv.at[t, i], (t, latent),
        ).wait_recv()

    def code_grad(i):
        rows = pl.ds(*GROUPS[i])
        back = lax.dot_general(
            err[rows, :], wd[...].reshape(LAYERS * BLOCK, D),
            (((1,), (1,)), ((), ())), preferred_element_type=jnp.float32,
        )
        grad[rows, :] = back
        grad_bf[rows, :] = back.astype(jnp.bfloat16)
        for s in range(LAYERS - 1):
            @pl.when(s < layer)
            def _(s=s):
                grad_copy(i, s).start()

    for j in range(CHUNKS):
        take_e(j, 2)

        @pl.when(middle == 1)
        def _(j=j):
            e_far[j].start()
            e_out[j, 3].start()

        take_e(j, 1)
    l_core.wait_recv()
    sum_chip[z] = sum_core[0] + sum_core[1]
    l_chip = [
        remote(sum_chip.at[z], sum_chip.at[z], l_send.at[m], l_recv.at[m], chip(m))
        for m in range(1, CHIPS)
    ]
    for copy in l_chip:
        copy.start()
    for m in (0, 1):
        for j in range(CHUNKS):
            ep_out[j, m].wait_recv()
    code_grad(0)
    for j in range(CHUNKS):
        ep_out[j, 2].wait_recv()
    code_grad(1)
    for copy in l_chip:
        copy.wait_recv()
    sum_layer[layer] = functools.reduce(jnp.add, [sum_chip[i] for i in range(CHIPS)])
    l_layer = [
        remote(
            sum_layer.at[layer], sum_layer.at[layer],
            l_send.at[CHIPS - 1 + d], l_recv.at[CHIPS - 1 + d],
            (lax.rem(layer + d, LAYERS), latent),
        )
        for d in range(1, LAYERS)
    ]
    for copy in l_layer:
        copy.start()
    for j in range(CHUNKS):
        take_e(j, 3)
    for j in range(CHUNKS):
        ep_out[j, 3].wait_recv()
    code_grad(2)

    for s in range(LAYERS):
        dec_g[s, 0] = lax.dot_general(
            codes[:, s * BLOCK:(s + 1) * BLOCK], err[...],
            (((0,), (0,)), ((), ())), preferred_element_type=jnp.float32,
        ).astype(jnp.bfloat16)

    acc[...] = grad[:, own_cols]
    for t in range(1, LAYERS):
        @pl.when(t > layer)
        def _(t=t):
            for i in range(len(GROUPS)):
                grad_wait(i, t)
            acc[...] += grad_in[t].astype(jnp.float32)
    pre_grad = jnp.where(masked[...] > 0, acc[...], 0.0)
    bias_g[...] = jnp.sum(pre_grad, axis=0, keepdims=True)
    enc_g[0] = jnp.dot(
        xt[...], pre_grad.astype(jnp.bfloat16), preferred_element_type=jnp.float32
    ).astype(jnp.bfloat16)

    for copy in l_layer:
        copy.wait_recv()
    every = functools.reduce(jnp.add, [sum_layer[i] for i in range(LAYERS)])
    loss[...] = jnp.sum(every, keepdims=True)

    for m in (1, 2):
        x_out[m].wait_send()
        for j in range(CHUNKS):
            e_out[j, m].wait_send()

    @pl.when(middle == 1)
    def _():
        for copy in [x_far, x_out[3], *e_far.values(), *[e_out[j, 3] for j in range(CHUNKS)]]:
            copy.wait_send()

    for copies in (xp_out, p_out, s_out, ep_out):
        for copy in copies.values():
            copy.wait_send()
    for copy in [l_core, *l_chip, *l_layer]:
        copy.wait_send()
    for t in range(LAYERS):
        @pl.when(t > layer)
        def _(t=t):
            for q in range(CHIPS):
                code_copy(q, t).wait_send()

        @pl.when(t < layer)
        def _(t=t):
            for i in range(len(GROUPS)):
                grad_copy(i, t).wait_send()


def fused(residual, target, enc_weight, enc_bias, dec_weight, active):
    bf, f32 = jnp.bfloat16, jnp.float32
    vmem, dma = pltpu.VMEM, pltpu.SemaphoreType.DMA
    in_hbm = pl.BlockSpec(memory_space=pltpu.HBM)
    in_vmem = pl.BlockSpec(memory_space=pltpu.VMEM)
    loss, enc_grad, bias_grad, dec_grad = pl.pallas_call(
        fused_kernel,
        out_shape=[
            jax.ShapeDtypeStruct((1, 1), f32),
            jax.ShapeDtypeStruct(enc_weight.shape, bf),
            jax.ShapeDtypeStruct(enc_bias.shape, f32),
            jax.ShapeDtypeStruct(dec_weight.shape, bf),
        ],
        in_specs=[in_hbm] * 5 + [pl.BlockSpec(memory_space=pltpu.SMEM)],
        out_specs=[in_vmem] * 4,
        scratch_shapes=[
            vmem((TOKENS, D), bf),
            vmem((D, TOKENS), bf),
            vmem((D, BLOCK), bf),
            vmem((LAYERS, BLOCK, D), bf),
            vmem((TILE, D), bf),
            vmem((1, BLOCK), f32),
            vmem((TOKENS, BLOCK), f32),
            vmem((TOKENS, LAYERS * BLOCK), bf),
            vmem((2, CHUNKS, 2, 2, TILE, CW), bf),
            vmem((2, CHUNKS, 2, TILE, CW), bf),
            vmem((CHUNKS, CHIPS, TILE, CW), bf),
            vmem((CHUNKS, CHIPS, TILE, CW), bf),
            vmem((TOKENS, D), bf),
            vmem((TOKENS, LAYERS * BLOCK), f32),
            vmem((TOKENS, LAYERS * BLOCK), bf),
            vmem((LAYERS, TOKENS, BLOCK), bf),
            vmem((TOKENS, BLOCK), f32),
            vmem((2, 8, 128), f32),
            vmem((CHIPS, 8, 128), f32),
            vmem((LAYERS, 8, 128), f32),
            dma((5,)),
            dma((CHIPS,)),
            dma((CHIPS,)),
            dma((CHIPS,)),
            dma((CHIPS,)),
            dma((LAYERS, CHIPS)),
            dma((LAYERS, CHIPS)),
            dma((2, CHUNKS)),
            dma((2, CHUNKS)),
            dma((CHUNKS, CHIPS)),
            dma((CHUNKS, CHIPS)),
            dma((CHUNKS, CHIPS)),
            dma((CHUNKS, CHIPS)),
            dma((CHUNKS, CHIPS)),
            dma((CHUNKS, CHIPS)),
            dma((LAYERS, len(GROUPS))),
            dma((LAYERS, len(GROUPS))),
            dma((CHIPS + LAYERS - 1,)),
            dma((CHIPS + LAYERS - 1,)),
        ],
        compiler_params=pltpu.CompilerParams(
            collective_id=0, has_side_effects=True, vmem_limit_bytes=47 * 2**20
        ),
        cost_estimate=pl.CostEstimate(
            flops=14 * 2 * TOKENS * D * BLOCK, bytes_accessed=10 * 2**20, transcendentals=0
        ),
        name="transcoder_step",
    )(residual, target, enc_weight, enc_bias, dec_weight, jnp.swapaxes(active, 1, 2))
    return (
        loss[0, 0] * (0.5 / (LAYERS * TOKENS * D)),
        enc_grad * jnp.asarray(1.0 / TILE, bf),
        bias_grad * (1.0 / TILE),
        dec_grad * jnp.asarray(1.0 / TILE, bf),
    )


def shifted(value, axis, steps):
    count = lax.axis_size(axis)
    leading, last = (max(0, -steps), min(count, count - steps))
    return lax.ppermute(value, axis, [(source, source + steps) for source in range(leading, last)])


def slot_list(active, layer, my_block, slot_count):
    block_ids = lax.dynamic_index_in_dim(active, layer, 0, keepdims=False)
    hit = jnp.any(block_ids == my_block, axis=1).astype(jnp.int32)
    every = jnp.arange(NTILE, dtype=jnp.int32)
    place = jnp.cumsum(hit) - 1
    chosen = (hit[None, :] == 1) & (
        place[None, :] == jnp.arange(slot_count, dtype=jnp.int32)[:, None]
    )
    tile_ids = jnp.sum(jnp.where(chosen, every[None, :], 0), axis=1)
    filled = jnp.sum(chosen.astype(jnp.float32), axis=1)
    return (tile_ids, filled)


def shards(residual, target, enc_weight, enc_bias, dec_weight, active):
    layers = dec_weight.shape[0]
    feat_dev = enc_weight.shape[2]
    layer_index = lax.axis_index("layer")
    my_block = lax.axis_index("latent") * feat_dev // BLOCK
    slot_count = CAP
    slot_rows = slot_count * TILE
    full_inputs = lax.all_gather(residual[0], "latent", axis=0, tiled=True).reshape(NTILE, TILE, D)
    own_tiles, own_filled = slot_list(active, layer_index, my_block, slot_count)
    rows = jnp.take(full_inputs, own_tiles, axis=0).reshape(slot_rows, D)
    preact = jnp.dot(rows, enc_weight[0], preferred_element_type=jnp.float32) + enc_bias[0][None, :]
    live = jnp.repeat(own_filled, TILE)[:, None]
    sparse_codes = (jnp.maximum(preact, 0.0) * live).astype(jnp.bfloat16)
    dec_all = dec_weight[:, 0]

    def take_source(carry, portion, source):
        writes, kept = carry
        usable = (source >= 0) & (source <= layer_index)
        source_idx = jnp.clip(source, 0, layers - 1)
        portion = jnp.where(usable, portion, jnp.zeros_like(portion))
        tile_ids, _ = slot_list(active, source_idx, my_block, slot_count)
        weight = lax.dynamic_index_in_dim(dec_all, source_idx, 0, keepdims=False)
        product = jnp.dot(portion, weight, preferred_element_type=jnp.float32).reshape(
            slot_count, TILE, D
        )
        writes = writes.at[tile_ids].add(product)
        kept = jnp.where(usable, kept.at[source_idx].set(portion), kept)
        return (writes, kept)

    start_state = (
        jnp.zeros((NTILE, TILE, D), jnp.float32),
        jnp.zeros((layers, slot_rows, feat_dev), jnp.bfloat16),
    )
    state = take_source(start_state, sparse_codes, layer_index)
    moving = sparse_codes
    for hop in range(1, layers):
        moving = shifted(moving, "layer", 1)
        state = take_source(state, moving, layer_index - hop)
    writes, kept = state
    recon = lax.psum_scatter(
        writes.reshape(NTILE * TILE, D), "latent", scatter_dimension=0, tiled=True
    )
    errors = recon - target[0].astype(jnp.float32)
    total = lax.psum(jnp.sum(errors * errors), ("layer", "latent"))
    loss = 0.5 * total / (layers * NTILE * TILE * D)
    full_errors = lax.all_gather(errors.astype(jnp.bfloat16), "latent", axis=0, tiled=True).reshape(
        NTILE, TILE, D
    )
    dec_grads = []
    code_grads = []
    for source in range(layers):
        tile_ids, _ = slot_list(active, source, my_block, slot_count)
        error_part = jnp.take(full_errors, tile_ids, axis=0).reshape(slot_rows, D)
        grad = lax.dot_general(
            kept[source], error_part, (((0,), (0,)), ((), ())), preferred_element_type=jnp.float32
        )
        dec_grads.append((grad / TILE).astype(jnp.bfloat16))
        back = lax.dot_general(
            error_part,
            dec_all[source],
            (((1,), (1,)), ((), ())),
            preferred_element_type=jnp.float32,
        )
        code_grads.append(jnp.where(source <= layer_index, back, jnp.zeros_like(back)))
    dec_grad = jnp.stack(dec_grads)[:, None]
    code_grad = jnp.stack(code_grads)
    running = code_grad
    for hop in range(1, layers):
        running = code_grad + shifted(running, "layer", -1)
    mine = lax.dynamic_index_in_dim(running, layer_index, 0, keepdims=False)
    pre_grad = jnp.where(preact > 0, mine, jnp.zeros_like(mine)) * live
    bias_grad = (jnp.sum(pre_grad, axis=0) / TILE)[None]
    enc_term = lax.dot_general(
        rows,
        pre_grad.astype(jnp.bfloat16),
        (((0,), (0,)), ((), ())),
        preferred_element_type=jnp.float32,
    )
    enc_grad = (enc_term / TILE).astype(jnp.bfloat16)[None]
    return (loss, enc_grad, bias_grad, dec_grad)


def solution(mesh):
    in_specs = (
        P("layer", "latent", None),
        P("layer", "latent", None),
        P("layer", None, "latent"),
        P("layer", "latent"),
        P(None, "layer", "latent", None),
        P(),
    )
    out_specs = (
        P(),
        P("layer", None, "latent"),
        P("layer", "latent"),
        P(None, "layer", "latent", None),
    )
    one_tile_each = mesh.shape["latent"] == NTILE and mesh.shape["layer"] == LAYERS
    step = fused if one_tile_each else shards
    return jax.shard_map(step, mesh=mesh, in_specs=in_specs, out_specs=out_specs, check_vma=False)
```

time: 111 us -> 89.3 us (0.80)
  Pallas kernels: 96 us -> 77.7 us
  local copies, waits for them, and re-layouts: 11.9 us -> 4.42 us
  other arithmetic: 0 us -> 3.72 us
    pallas_call x1, Pallas kernels: 96 us -> 77.7 us  [fused(): pl.pallas_call(fused_kernel, out_shape=[jax.ShapeDtypeStruct((1, 1), f32)...]
    unnamed x14 -> x10, local copies, waits for them, and re-layouts: 11.9 us -> 4.42 us
    mul x0 -> x3, other arithmetic: none -> 3.72 us  [the longest x1 2.15 us: fused(): dec_grad * jnp.asarray(1.0 / TILE, bf)]
where the time goes in v2:
time: 89.3 us; the launch traced here: 88.2 us
  Pallas kernels  77.7 us (87%)
  local copies, waits for them, and re-layouts  4.42 us (5%)
  other arithmetic  3.72 us (4%)
  between operations  2.34 us (3%)
    pallas_call x1, Pallas kernels, fused(): pl.pallas_call(fused_kernel, out_shape=[jax.ShapeDtypeStruct((1, 1), f32)...  77.7 us
    unnamed x10, local copies, waits for them, and re-layouts  4.42 us
    mul x1, other arithmetic, fused(): dec_grad * jnp.asarray(1.0 / TILE, bf)  2.15 us

profile of v2, /device:TPU:0, one launch (start us, length us, event | category | flops | bytes accessed | tf_op | source)
XLA Modules:
  0.0 88.2 jit_solution(3659748259918826806)
XLA Ops:
  0.6 0.0 copy-start
  0.6 1.2 %copy-done = bf16[1,1792,256]{2,1,0:T(8,128)(2,1)S(1)} copy-done((bf16[1,1792,256]{2,1,0:T(8,128)(2,1)S(1)}, bf16[1,1792,256]{2,1,0:T(8,128)(2,1)}, u32[]{:S(2)}) %copy-start) | copy-done | bytes 917528
  1.8 0.0 copy-start.1
  1.8 0.9 %copy-done.1 = bf16[1,64,1792]{2,1,0:T(8,128)(2,1)S(1)} copy-done((bf16[1,64,1792]{2,1,0:T(8,128)(2,1)S(1)}, bf16[1,64,1792]{2,1,0:T(8,128)(2,1)}, u32[]{:S(2)}) %copy-start.1) | copy-done | bytes 229400
  2.8 0.0 copy-start.2
  2.8 0.9 %copy-done.2 = bf16[1,64,1792]{2,1,0:T(8,128)(2,1)S(1)} copy-done((bf16[1,64,1792]{2,1,0:T(8,128)(2,1)S(1)}, bf16[1,64,1792]{2,1,0:T(8,128)(2,1)}, u32[]{:S(2)}) %copy-start.2) | copy-done | bytes 229400
  3.7 0.0 copy-start.3
  3.7 0.7 copy-done.3
  4.4 0.0 copy-start.4
  4.4 0.7 copy-done.4
  5.1 77.7 %transcoder_step.1 = (f32[1,1]{1,0:T(1,128)}, bf16[1,1792,256]{2,1,0:T(8,128)(2,1)S(1)}, f32[1,256]{1,0:T(1,128)S(1)}, bf16[4,1,256,1792]{3,2,1,0:T(8,128)(2,1)S(1)}) custom-call(bf16[1,64,1792]{2,1,0:T(8,128)(2,1)S(1)} %copy-done.1, bf16[1,64,1792]{2,1,0:T(8,128)(2,1)S(1)} %copy-done.2, bf16[1,1792,256]{2,1,0:T(8,128)(2,1)S(1)} %copy-done, ...), custom_call_target="tpu_custom_call" | custom-call | flops 6576668672 | bytes 10485760 | tf_op jit(solution)/shard_map/transcoder_step/pallas_call | solution.py:385
  83.3 1.0 %broadcast_multiply_fusion.1 = bf16[1,1792,256]{2,1,0:T(8,128)(2,1)} fusion(bf16[1,1792,256]{2,1,0:T(8,128)(2,1)S(1)} %get-tuple-element.9), kind=kLoop, calls=%fused_computation.1 | loop fusion | flops 458752 | bytes 1835008 | tf_op jit(solution)/shard_map/mul | solution.py:446
  84.3 0.6 broadcast_multiply_fusion.2
  84.9 2.2 %broadcast_multiply_fusion = bf16[4,1,256,1792]{3,2,1,0:T(8,128)(2,1)} fusion(bf16[4,1,256,1792]{3,2,1,0:T(8,128)(2,1)S(1)} %get-tuple-element.11), kind=kLoop, calls=%fused_computation | loop fusion | flops 1835008 | bytes 7340032 | tf_op jit(solution)/shard_map/mul | solution.py:448
Async XLA Ops:
  0.6 1.2 %copy-start = (bf16[1,1792,256]{2,1,0:T(8,128)(2,1)S(1)}, bf16[1,1792,256]{2,1,0:T(8,128)(2,1)}, u32[]{:S(2)}) copy-start(bf16[1,1792,256]{2,1,0:T(8,128)(2,1)} %enc_w.1) | copy-start | bytes 2752516
  1.8 0.9 %copy-start.1 = (bf16[1,64,1792]{2,1,0:T(8,128)(2,1)S(1)}, bf16[1,64,1792]{2,1,0:T(8,128)(2,1)}, u32[]{:S(2)}) copy-start(bf16[1,64,1792]{2,1,0:T(8,128)(2,1)} %res.1) | copy-start | bytes 688132
  2.8 0.9 %copy-start.2 = (bf16[1,64,1792]{2,1,0:T(8,128)(2,1)S(1)}, bf16[1,64,1792]{2,1,0:T(8,128)(2,1)}, u32[]{:S(2)}) copy-start(bf16[1,64,1792]{2,1,0:T(8,128)(2,1)} %tgt.1) | copy-start | bytes 688132
  3.7 0.7 copy-start.3
  4.4 0.7 copy-start.4

commit v3 on v2

--- a/solution.py
+++ b/solution.py
@@ -26,8 +26,8 @@
     res, tgt, enc_w, bias, dec_w, active,
     loss, enc_g, bias_g, dec_g,
     x, xt, we, wd, goal, offset, masked, codes, part, part_in, shares, share_in, err,
-    grad, grad_bf, grad_in, acc, sum_core, sum_chip, sum_layer,
-    load_sem, x_send, x_recv, xp_send, xp_recv, c_send, c_recv,
+    grad, grad_bf, grad_in, acc, dec_v, enc_v, sum_core, sum_chip, sum_layer,
+    load_sem, store_sem, x_send, x_recv, xp_send, xp_recv, c_send, c_recv,
     p_send, p_recv, s_send, s_recv, e_send, e_recv, ep_send, ep_recv, g_send, g_recv,
     l_send, l_recv,
 ):
@@ -128,24 +128,27 @@
 
     p_out, s_out = {}, {}
 
-    def decode(g, j):
-        full = jnp.dot(
-            codes[g * 2 * PAIR:(g + 1) * 2 * PAIR, :],
-            wd[:, :, j * CW:(j + 1) * CW].reshape(LAYERS * BLOCK, CW),
-            preferred_element_type=jnp.float32,
-        ).astype(jnp.bfloat16)
-        for q in range(2):
-            for c in range(2):
-                at = q * PAIR + c * TILE
-                part[g, j, c, q] = full[at:at + TILE]
-        p_out[g, j] = remote(
-            part.at[g, j, 1 - core], part_in.at[g, j], p_send.at[g, j], p_recv.at[g, j], partner
-        )
-        p_out[g, j].start()
+    def decode(first, count):
+        for j in range(CHUNKS):
+            full = jnp.dot(
+                codes[first * PAIR:(first + count) * PAIR, :],
+                wd[:, :, j * CW:(j + 1) * CW].reshape(LAYERS * BLOCK, CW),
+                preferred_element_type=jnp.float32,
+            ).astype(jnp.bfloat16)
+            for q in range(count):
+                for c in range(2):
+                    at = q * PAIR + c * TILE
+                    part[first + q, c, :, j * CW:(j + 1) * CW] = full[at:at + TILE]
+        for q in range(first, first + count):
+            p_out[q] = remote(
+                part.at[q, 1 - core], part_in.at[q], p_send.at[q], p_recv.at[q], partner
+            )
+            p_out[q].start()
 
     def chip_sum(j, m):
-        own = part[m // 2, j, core, m % 2].astype(jnp.float32)
-        return own + part_in[m // 2, j, m % 2].astype(jnp.float32)
+        cols = slice(j * CW, (j + 1) * CW)
+        own = part[m, core, :, cols].astype(jnp.float32)
+        return own + part_in[m, :, cols].astype(jnp.float32)
 
     def send_share(j, m, slot, device):
         s_out[j, m] = remote(
@@ -179,37 +182,44 @@
     loads[3].wait()
     code_wait(0)
     code_wait(1)
-    for j in range(CHUNKS):
-        decode(0, j)
+    decode(0, 2)
     take_x(3)
-    for j in range(CHUNKS):
-        p_out[0, j].wait_recv()
+    p_out[0].wait_recv()
+    p_out[1].wait_recv()
+    for j in range(CHUNKS):
         shares[j, 1] = chip_sum(j, 1).astype(jnp.bfloat16)
         send_share(j, 1, 1, chip(1))
+    code_wait(2)
+    decode(2, 1)
     xp_out[3].wait_recv()
     encode(3)
-    code_wait(2)
+    p_out[2].wait_recv()
+    for j in range(CHUNKS):
+        shares[j, 2] = chip_sum(j, 2).astype(jnp.bfloat16)
+        s_out[j, 2] = remote(
+            shares.at[j, 2], share_in.at[j, 2], s_send.at[j, 2], s_recv.at[j, 2], chip(2)
+        )
+
+        @pl.when(middle == 0)
+        def _(j=j):
+            s_out[j, 2].start()
+
     code_wait(3)
-    for j in range(CHUNKS):
-        decode(1, j)
+    decode(3, 1)
     far = (layer, 2 * (middle * mates[3] + (1 - middle) * mates[1]) + core)
-    for j in range(CHUNKS):
-        p_out[1, j].wait_recv()
+    p_out[3].wait_recv()
+    for j in range(CHUNKS):
         shares[j, 3] = chip_sum(j, 3).astype(jnp.bfloat16)
         send_share(j, 3, 3 * middle, far)
-    for j in range(CHUNKS):
-        @pl.when(middle == 0)
-        def _(j=j):
-            shares[j, 2] = chip_sum(j, 2).astype(jnp.bfloat16)
-
-        @pl.when(middle == 1)
-        def _(j=j):
+
+    @pl.when(middle == 1)
+    def _():
+        for j in range(CHUNKS):
             share_wait(j, 0)
             shares[j, 2] = (
                 chip_sum(j, 2) + share_in[j, 0].astype(jnp.float32)
             ).astype(jnp.bfloat16)
-
-        send_share(j, 2, 2, chip(2))
+            s_out[j, 2].start()
 
     xt[...] = x[...].T
 
@@ -326,11 +336,14 @@
         ep_out[j, 3].wait_recv()
     code_grad(2)
 
+    stores = []
     for s in range(LAYERS):
-        dec_g[s, 0] = lax.dot_general(
+        dec_v[s] = lax.dot_general(
             codes[:, s * BLOCK:(s + 1) * BLOCK], err[...],
             (((0,), (0,)), ((), ())), preferred_element_type=jnp.float32,
         ).astype(jnp.bfloat16)
+        stores.append(pltpu.make_async_copy(dec_v.at[s], dec_g.at[s, 0], store_sem.at[s]))
+        stores[s].start()
 
     acc[...] = grad[:, own_cols]
     for t in range(1, LAYERS):
@@ -341,9 +354,11 @@
             acc[...] += grad_in[t].astype(jnp.float32)
     pre_grad = jnp.where(masked[...] > 0, acc[...], 0.0)
     bias_g[...] = jnp.sum(pre_grad, axis=0, keepdims=True)
-    enc_g[0] = jnp.dot(
+    enc_v[...] = jnp.dot(
         xt[...], pre_grad.astype(jnp.bfloat16), preferred_element_type=jnp.float32
     ).astype(jnp.bfloat16)
+    stores.append(pltpu.make_async_copy(enc_v, enc_g.at[0], store_sem.at[LAYERS]))
+    stores[LAYERS].start()
 
     for copy in l_layer:
         copy.wait_recv()
@@ -375,6 +390,8 @@
         def _(t=t):
             for i in range(len(GROUPS)):
                 grad_copy(i, t).wait_send()
+    for store in stores:
+        store.wait()
 
 
 def fused(residual, target, enc_weight, enc_bias, dec_weight, active):
@@ -391,7 +408,7 @@
             jax.ShapeDtypeStruct(dec_weight.shape, bf),
         ],
         in_specs=[in_hbm] * 5 + [pl.BlockSpec(memory_space=pltpu.SMEM)],
-        out_specs=[in_vmem] * 4,
+        out_specs=[in_vmem, in_hbm, in_vmem, in_hbm],
         scratch_shapes=[
             vmem((TOKENS, D), bf),
             vmem((D, TOKENS), bf),
@@ -401,8 +418,8 @@
             vmem((1, BLOCK), f32),
             vmem((TOKENS, BLOCK), f32),
             vmem((TOKENS, LAYERS * BLOCK), bf),
-            vmem((2, CHUNKS, 2, 2, TILE, CW), bf),
-            vmem((2, CHUNKS, 2, TILE, CW), bf),
+            vmem((CHIPS, 2, TILE, D), bf),
+            vmem((CHIPS, TILE, D), bf),
             vmem((CHUNKS, CHIPS, TILE, CW), bf),
             vmem((CHUNKS, CHIPS, TILE, CW), bf),
             vmem((TOKENS, D), bf),
@@ -410,18 +427,21 @@
             vmem((TOKENS, LAYERS * BLOCK), bf),
             vmem((LAYERS, TOKENS, BLOCK), bf),
             vmem((TOKENS, BLOCK), f32),
+            vmem((LAYERS, BLOCK, D), bf),
+            vmem((D, BLOCK), bf),
             vmem((2, 8, 128), f32),
             vmem((CHIPS, 8, 128), f32),
             vmem((LAYERS, 8, 128), f32),
             dma((5,)),
+            dma((LAYERS + 1,)),
             dma((CHIPS,)),
             dma((CHIPS,)),
             dma((CHIPS,)),
             dma((CHIPS,)),
             dma((LAYERS, CHIPS)),
             dma((LAYERS, CHIPS)),
-            dma((2, CHUNKS)),
-            dma((2, CHUNKS)),
+            dma((CHIPS,)),
+            dma((CHIPS,)),
             dma((CHUNKS, CHIPS)),
             dma((CHUNKS, CHIPS)),
             dma((CHUNKS, CHIPS)),
@@ -434,7 +454,7 @@
             dma((CHIPS + LAYERS - 1,)),
         ],
         compiler_params=pltpu.CompilerParams(
-            collective_id=0, has_side_effects=True, vmem_limit_bytes=47 * 2**20
+            collective_id=0, has_side_effects=True, vmem_limit_bytes=56 * 2**20
         ),
         cost_estimate=pl.CostEstimate(
             flops=14 * 2 * TOKENS * D * BLOCK, bytes_accessed=10 * 2**20, transcendentals=0

time: 89.3 us -> 89.9 us (level)
  local copies, waits for them, and re-layouts: 4.42 us -> 0 us
  other arithmetic: 3.72 us -> 7.6 us
  Pallas kernels: 77.7 us -> 79.6 us
    unnamed x10 -> x0, local copies, waits for them, and re-layouts: 4.42 us -> none
    mul x1, other arithmetic: 2.15 us -> 4.19 us  [fused(): dec_grad * jnp.asarray(1.0 / TILE, bf)]
    pallas_call x1, Pallas kernels: 77.7 us -> 79.6 us  [fused(): pl.pallas_call(fused_kernel, out_shape=[jax.ShapeDtypeStruct((1, 1), f32)...]
    mul x1, other arithmetic: 1 us -> 2.18 us  [fused(): enc_grad * jnp.asarray(1.0 / TILE, bf)]
where the time goes in v3:
time: 89.9 us; the launch traced here: 89.6 us
  Pallas kernels  79.6 us (89%)
  other arithmetic  7.6 us (8%)
  between operations  2.39 us (3%)
    pallas_call x1, Pallas kernels, fused(): pl.pallas_call(fused_kernel, out_shape=[jax.ShapeDtypeStruct((1, 1), f32)...  79.6 us
    mul x1, other arithmetic, fused(): dec_grad * jnp.asarray(1.0 / TILE, bf)  4.19 us
    mul x1, other arithmetic, fused(): enc_grad * jnp.asarray(1.0 / TILE, bf)  2.18 us

profile of v3, /device:TPU:0, one launch (start us, length us, event | category | flops | bytes accessed | tf_op | source)
XLA Modules:
  0.0 89.6 jit_solution(15771227921460130793)
XLA Ops:
  0.6 79.6 %transcoder_step.1 = (f32[1,1]{1,0:T(1,128)}, bf16[1,1792,256]{2,1,0:T(8,128)(2,1)}, f32[1,256]{1,0:T(1,128)}, bf16[4,1,256,1792]{3,2,1,0:T(8,128)(2,1)}) custom-call(bf16[1,64,1792]{2,1,0:T(8,128)(2,1)} %res.1, bf16[1,64,1792]{2,1,0:T(8,128)(2,1)} %tgt.1, bf16[1,1792,256]{2,1,0:T(8,128)(2,1)} %enc_w.1, f32[1,256]{1,0:T(1,128)} %bias.1, ...), custom_call_target="tpu_custom_call" | custom-call | flops 6576668672 | bytes 10485760 | tf_op jit(solution)/shard_map/transcoder_step/pallas_call | solution.py:402
  80.9 2.2 %broadcast_multiply_fusion.1 = bf16[1,1792,256]{2,1,0:T(8,128)(2,1)} fusion(bf16[1,1792,256]{2,1,0:T(8,128)(2,1)} %get-tuple-element.9), kind=kLoop, calls=%fused_computation.1 | loop fusion | flops 458752 | bytes 1835008 | tf_op jit(solution)/shard_map/mul | solution.py:466
  83.1 1.2 %broadcast_multiply_fusion.2 = f32[1,256]{1,0:T(1,128)} fusion(f32[1,256]{1,0:T(1,128)} %get-tuple-element.10), kind=kLoop, calls=%fused_computation.2 | loop fusion | flops 256 | bytes 2048 | tf_op jit(solution)/shard_map/mul | solution.py:467
  84.3 4.2 %broadcast_multiply_fusion = bf16[4,1,256,1792]{3,2,1,0:T(8,128)(2,1)} fusion(bf16[4,1,256,1792]{3,2,1,0:T(8,128)(2,1)} %get-tuple-element.11), kind=kLoop, calls=%fused_computation | loop fusion | flops 1835008 | bytes 7340032 | tf_op jit(solution)/shard_map/mul | solution.py:468

commit v4 on v3

--- a/solution.py
+++ b/solution.py
@@ -26,8 +26,8 @@
     res, tgt, enc_w, bias, dec_w, active,
     loss, enc_g, bias_g, dec_g,
     x, xt, we, wd, goal, offset, masked, codes, part, part_in, shares, share_in, err,
-    grad, grad_bf, grad_in, acc, dec_v, enc_v, sum_core, sum_chip, sum_layer,
-    load_sem, store_sem, x_send, x_recv, xp_send, xp_recv, c_send, c_recv,
+    grad, grad_bf, grad_in, acc, dec_acc, sum_core, sum_chip, sum_layer,
+    load_sem, x_send, x_recv, xp_send, xp_recv, c_send, c_recv,
     p_send, p_recv, s_send, s_recv, e_send, e_recv, ep_send, ep_recv, g_send, g_recv,
     l_send, l_recv,
 ):
@@ -293,6 +293,12 @@
             def _(s=s):
                 grad_copy(i, s).start()
 
+    def dec_term(s, first, count):
+        return lax.dot_general(
+            codes[first:first + count, s * BLOCK:(s + 1) * BLOCK], err[first:first + count, :],
+            (((0,), (0,)), ((), ())), preferred_element_type=jnp.float32,
+        )
+
     for j in range(CHUNKS):
         take_e(j, 2)
 
@@ -330,20 +336,21 @@
     ]
     for copy in l_layer:
         copy.start()
+    dec_acc[0] = dec_term(0, 0, 3 * PAIR)
+    dec_acc[1] = dec_term(1, 0, 3 * PAIR)
     for j in range(CHUNKS):
         take_e(j, 3)
+    dec_acc[2] = dec_term(2, 0, 3 * PAIR)
     for j in range(CHUNKS):
         ep_out[j, 3].wait_recv()
     code_grad(2)
 
-    stores = []
     for s in range(LAYERS):
-        dec_v[s] = lax.dot_general(
-            codes[:, s * BLOCK:(s + 1) * BLOCK], err[...],
-            (((0,), (0,)), ((), ())), preferred_element_type=jnp.float32,
-        ).astype(jnp.bfloat16)
-        stores.append(pltpu.make_async_copy(dec_v.at[s], dec_g.at[s, 0], store_sem.at[s]))
-        stores[s].start()
+        if s < 3:
+            total = dec_acc[s] + dec_term(s, 3 * PAIR, PAIR)
+        else:
+            total = dec_term(s, 0, TOKENS)
+        dec_g[s, 0] = total.astype(jnp.bfloat16)
 
     acc[...] = grad[:, own_cols]
     for t in range(1, LAYERS):
@@ -354,11 +361,9 @@
             acc[...] += grad_in[t].astype(jnp.float32)
     pre_grad = jnp.where(masked[...] > 0, acc[...], 0.0)
     bias_g[...] = jnp.sum(pre_grad, axis=0, keepdims=True)
-    enc_v[...] = jnp.dot(
+    enc_g[0] = jnp.dot(
         xt[...], pre_grad.astype(jnp.bfloat16), preferred_element_type=jnp.float32
     ).astype(jnp.bfloat16)
-    stores.append(pltpu.make_async_copy(enc_v, enc_g.at[0], store_sem.at[LAYERS]))
-    stores[LAYERS].start()
 
     for copy in l_layer:
         copy.wait_recv()
@@ -390,8 +395,6 @@
         def _(t=t):
             for i in range(len(GROUPS)):
                 grad_copy(i, t).wait_send()
-    for store in stores:
-        store.wait()
 
 
 def fused(residual, target, enc_weight, enc_bias, dec_weight, active):
@@ -408,7 +411,7 @@
             jax.ShapeDtypeStruct(dec_weight.shape, bf),
         ],
         in_specs=[in_hbm] * 5 + [pl.BlockSpec(memory_space=pltpu.SMEM)],
-        out_specs=[in_vmem, in_hbm, in_vmem, in_hbm],
+        out_specs=[in_vmem] * 4,
         scratch_shapes=[
             vmem((TOKENS, D), bf),
             vmem((D, TOKENS), bf),
@@ -427,13 +430,11 @@
             vmem((TOKENS, LAYERS * BLOCK), bf),
             vmem((LAYERS, TOKENS, BLOCK), bf),
             vmem((TOKENS, BLOCK), f32),
-            vmem((LAYERS, BLOCK, D), bf),
-            vmem((D, BLOCK), bf),
+            vmem((3, BLOCK, D), f32),
             vmem((2, 8, 128), f32),
             vmem((CHIPS, 8, 128), f32),
             vmem((LAYERS, 8, 128), f32),
             dma((5,)),
-            dma((LAYERS + 1,)),
             dma((CHIPS,)),
             dma((CHIPS,)),
             dma((CHIPS,)),
@@ -454,7 +455,7 @@
             dma((CHIPS + LAYERS - 1,)),
         ],
         compiler_params=pltpu.CompilerParams(
-            collective_id=0, has_side_effects=True, vmem_limit_bytes=56 * 2**20
+            collective_id=0, has_side_effects=True, vmem_limit_bytes=47 * 2**20
         ),
         cost_estimate=pl.CostEstimate(
             flops=14 * 2 * TOKENS * D * BLOCK, bytes_accessed=10 * 2**20, transcendentals=0

time: 89.9 us -> 89.6 us (level)
  local copies, waits for them, and re-layouts: 0 us -> 4.42 us
  other arithmetic: 7.6 us -> 3.72 us
    unnamed x0 -> x10, local copies, waits for them, and re-layouts: none -> 4.42 us
    mul x1, other arithmetic: 4.19 us -> 2.15 us  [fused(): dec_grad * jnp.asarray(1.0 / TILE, bf)]
    mul x1, other arithmetic: 2.18 us -> 1 us  [fused(): enc_grad * jnp.asarray(1.0 / TILE, bf)]
where the time goes in v4:
time: 89.6 us; the launch traced here: 89.3 us
  Pallas kernels  78.8 us (88%)
  local copies, waits for them, and re-layouts  4.42 us (5%)
  other arithmetic  3.72 us (4%)
  between operations  2.34 us (3%)
    pallas_call x1, Pallas kernels, fused(): pl.pallas_call(fused_kernel, out_shape=[jax.ShapeDtypeStruct((1, 1), f32)...  78.8 us
    unnamed x10, local copies, waits for them, and re-layouts  4.42 us
    mul x1, other arithmetic, fused(): dec_grad * jnp.asarray(1.0 / TILE, bf)  2.15 us

profile of v4, /device:TPU:0, one launch (start us, length us, event | category | flops | bytes accessed | tf_op | source)
XLA Modules:
  0.0 89.3 jit_solution(3137336245415525913)
XLA Ops:
  0.6 0.0 copy-start
  0.6 1.2 %copy-done = bf16[1,1792,256]{2,1,0:T(8,128)(2,1)S(1)} copy-done((bf16[1,1792,256]{2,1,0:T(8,128)(2,1)S(1)}, bf16[1,1792,256]{2,1,0:T(8,128)(2,1)}, u32[]{:S(2)}) %copy-start) | copy-done | bytes 917528
  1.8 0.0 copy-start.1
  1.8 0.9 %copy-done.1 = bf16[1,64,1792]{2,1,0:T(8,128)(2,1)S(1)} copy-done((bf16[1,64,1792]{2,1,0:T(8,128)(2,1)S(1)}, bf16[1,64,1792]{2,1,0:T(8,128)(2,1)}, u32[]{:S(2)}) %copy-start.1) | copy-done | bytes 229400
  2.8 0.0 copy-start.2
  2.8 0.9 %copy-done.2 = bf16[1,64,1792]{2,1,0:T(8,128)(2,1)S(1)} copy-done((bf16[1,64,1792]{2,1,0:T(8,128)(2,1)S(1)}, bf16[1,64,1792]{2,1,0:T(8,128)(2,1)}, u32[]{:S(2)}) %copy-start.2) | copy-done | bytes 229400
  3.7 0.0 copy-start.3
  3.7 0.7 copy-done.3
  4.4 0.0 copy-start.4
  4.4 0.7 copy-done.4
  5.1 78.8 %transcoder_step.1 = (f32[1,1]{1,0:T(1,128)}, bf16[1,1792,256]{2,1,0:T(8,128)(2,1)S(1)}, f32[1,256]{1,0:T(1,128)S(1)}, bf16[4,1,256,1792]{3,2,1,0:T(8,128)(2,1)S(1)}) custom-call(bf16[1,64,1792]{2,1,0:T(8,128)(2,1)S(1)} %copy-done.1, bf16[1,64,1792]{2,1,0:T(8,128)(2,1)S(1)} %copy-done.2, bf16[1,1792,256]{2,1,0:T(8,128)(2,1)S(1)} %copy-done, ...), custom_call_target="tpu_custom_call" | custom-call | flops 6576668672 | bytes 10485760 | tf_op jit(solution)/shard_map/transcoder_step/pallas_call | solution.py:405
  84.5 1.0 %broadcast_multiply_fusion.1 = bf16[1,1792,256]{2,1,0:T(8,128)(2,1)} fusion(bf16[1,1792,256]{2,1,0:T(8,128)(2,1)S(1)} %get-tuple-element.9), kind=kLoop, calls=%fused_computation.1 | loop fusion | flops 458752 | bytes 1835008 | tf_op jit(solution)/shard_map/mul | solution.py:467
  85.5 0.6 broadcast_multiply_fusion.2
  86.0 2.2 %broadcast_multiply_fusion = bf16[4,1,256,1792]{3,2,1,0:T(8,128)(2,1)} fusion(bf16[4,1,256,1792]{3,2,1,0:T(8,128)(2,1)S(1)} %get-tuple-element.11), kind=kLoop, calls=%fused_computation | loop fusion | flops 1835008 | bytes 7340032 | tf_op jit(solution)/shard_map/mul | solution.py:469
Async XLA Ops:
  0.6 1.2 %copy-start = (bf16[1,1792,256]{2,1,0:T(8,128)(2,1)S(1)}, bf16[1,1792,256]{2,1,0:T(8,128)(2,1)}, u32[]{:S(2)}) copy-start(bf16[1,1792,256]{2,1,0:T(8,128)(2,1)} %enc_w.1) | copy-start | bytes 2752516
  1.8 0.9 %copy-start.1 = (bf16[1,64,1792]{2,1,0:T(8,128)(2,1)S(1)}, bf16[1,64,1792]{2,1,0:T(8,128)(2,1)}, u32[]{:S(2)}) copy-start(bf16[1,64,1792]{2,1,0:T(8,128)(2,1)} %res.1) | copy-start | bytes 688132
  2.8 0.9 %copy-start.2 = (bf16[1,64,1792]{2,1,0:T(8,128)(2,1)S(1)}, bf16[1,64,1792]{2,1,0:T(8,128)(2,1)}, u32[]{:S(2)}) copy-start(bf16[1,64,1792]{2,1,0:T(8,128)(2,1)} %tgt.1) | copy-start | bytes 688132
  3.7 0.7 copy-start.3
  4.4 0.7 copy-start.4
